TPU v7x, 256 devices: a whole 4x4x8 slice. The times are simulated.
256 devices in a mesh: grp: 8 (over y, core), blk: 32 (over z, x).
Axes of the slice: x: 4, y: 4, z: 8, core: 2. Of those that a mesh axis runs over, the one named last changes fastest.
Arguments:
- features: bfloat16 [524288, 128], P(('grp', 'blk')), may hold values from -6 to 6
- w_self: bfloat16 [128, 256], replicated, may hold values from -0.5 to 0.5
- w_neigh: bfloat16 [128, 256], replicated, may hold values from -0.5 to 0.5
- cotangent: bfloat16 [524288, 256], P(('grp', 'blk')), may hold values from -6 to 6
- src_block: int32 [256, 32, 4], P(('grp', 'blk')), may hold values from 0 to 15
- dst_block: int32 [256, 32, 4], P(('grp', 'blk')), may hold values from 0 to 127
- block_count: int32 [256, 32], P(('grp', 'blk')), may hold values from 0 to 4, as said below
- edge_rows: int32 [256, 32, 4, 192], P(('grp', 'blk')), may hold values from 0 to 127
- edge_cols: int32 [256, 32, 4, 192], P(('grp', 'blk')), may hold values from 0 to 127
Outputs:
- activated: bfloat16 [524288, 256], P(('grp', 'blk'))
- grad_features: bfloat16 [524288, 128], P(('grp', 'blk'))
- grad_self: float32 [128, 256], replicated
- grad_neigh: float32 [128, 256], replicated
Inputs may be any that keep to these rules, and one draw needn't show every extreme that they name: Slot c of sender d for owner o holds data when c < block_count[d, o]; entries of other slots are ignored. In every draw some owner receives 4 used slots from every device of its group. `dst_block`: the destination row block t of a slot to owner o is local block t % 16 of device (t // 16) * 32 + o.
All inputs are finite; a program needn't handle non-finite values.
Results may differ from a plain program's by a relative error of at most 0.0052.
Values may be sent and summed in bfloat16 or wider, within the bound.
No kernel may reach another device: no remote copies, remote signals or barrier semaphores. Data moves between devices by JAX's collectives and lax.ppermute only.
A program may use at most 64 MiB of HBM per device.

v0:
```python
import jax
import jax.numpy as jnp
from jax import lax
from jax.sharding import PartitionSpec as P

BS = 128


def one_hot(labels, extent):
    return (labels[..., None] == jnp.arange(extent, dtype=jnp.int32)).astype(jnp.bfloat16)


def on_device(
    features, w_self, w_neigh, cotangent, src_block, dst_block, block_count, edge_rows, edge_cols
):
    block_rows = BS
    owners = src_block.shape[1]
    capacity = src_block.shape[2]
    local_nodes = features.shape[0]
    local_blocks = local_nodes // block_rows
    groups = lax.axis_size("grp")
    node_total = local_nodes * groups * lax.axis_size("blk")
    src_local = src_block[0]
    dst_local = dst_block[0]
    in_use = lax.broadcasted_iota(jnp.int32, (owners, capacity), 1) < block_count[0][:, None]
    row_ids = jnp.where(in_use[..., None], edge_rows[0], block_rows)
    col_ids = jnp.where(in_use[..., None], edge_cols[0], block_rows)
    src_nodes = src_local[..., None] * block_rows + edge_cols[0]
    messages = jnp.where(in_use[..., None, None], features[src_nodes], jnp.zeros((), jnp.bfloat16))
    row_table = one_hot(row_ids, block_rows)
    row_sums = jnp.einsum(
        "oceb,ocef->ocbf", row_table, messages, preferred_element_type=jnp.float32
    )
    row_counts = jnp.sum(row_table, axis=2, dtype=jnp.float32)
    got_sums, got_counts, got_dst = (
        lax.all_to_all(row_sums, "blk", split_axis=0, concat_axis=0, tiled=True),
        lax.all_to_all(row_counts, "blk", split_axis=0, concat_axis=0, tiled=True),
        lax.all_to_all(dst_local, "blk", split_axis=0, concat_axis=0, tiled=True),
    )
    slot_total = owners * capacity
    targets = got_dst.reshape(slot_total)
    acc_sums = jax.ops.segment_sum(
        got_sums.reshape(slot_total, block_rows, -1), targets, groups * local_blocks
    )
    acc_counts = jax.ops.segment_sum(
        got_counts.reshape(slot_total, block_rows), targets, groups * local_blocks
    )
    own_sums, own_counts = (
        lax.psum_scatter(acc_sums, "grp", scatter_dimension=0, tiled=True),
        lax.psum_scatter(acc_counts, "grp", scatter_dimension=0, tiled=True),
    )
    divisor = jnp.maximum(own_counts, 1.0).reshape(local_nodes, 1)
    neigh_mean = (own_sums.reshape(local_nodes, -1) / divisor).astype(jnp.bfloat16)
    preact = jnp.dot(features, w_self, preferred_element_type=jnp.float32) + jnp.dot(
        neigh_mean, w_neigh, preferred_element_type=jnp.float32
    )
    sigmoids = jax.nn.sigmoid(preact)
    activated = (preact * sigmoids).astype(jnp.bfloat16)
    grad_pre = (
        cotangent.astype(jnp.float32) * sigmoids * (1.0 + preact * (1.0 - sigmoids))
    ).astype(jnp.bfloat16)
    local_self = jnp.einsum("nf,nh->fh", features, grad_pre, preferred_element_type=jnp.float32)
    local_neigh = jnp.einsum("nf,nh->fh", neigh_mean, grad_pre, preferred_element_type=jnp.float32)
    grad_self, grad_neigh = lax.psum((local_self, local_neigh), ("grp", "blk"))
    grad_scale = float(node_total) ** (-0.5)
    grad_self = grad_self * grad_scale
    grad_neigh = grad_neigh * grad_scale
    grad_mean = (
        jnp.einsum("nh,fh->nf", grad_pre, w_neigh, preferred_element_type=jnp.float32) / divisor
    ).astype(jnp.bfloat16)
    mean_all = lax.all_gather(
        grad_mean.reshape(local_blocks, block_rows, -1), "grp", axis=0, tiled=True
    )
    slot_grads = mean_all[got_dst]
    returned = lax.all_to_all(slot_grads, "blk", split_axis=0, concat_axis=0, tiled=True)
    picked = jnp.einsum(
        "oceb,ocbf->ocef", row_table, returned, preferred_element_type=jnp.float32
    ).astype(jnp.bfloat16)
    col_table = one_hot(col_ids, block_rows)
    col_sums = jnp.einsum("oceb,ocef->ocbf", col_table, picked, preferred_element_type=jnp.float32)
    spread = jax.ops.segment_sum(
        col_sums.reshape(slot_total, block_rows, -1), src_local.reshape(slot_total), local_blocks
    )
    own_term = jnp.einsum("nh,fh->nf", grad_pre, w_self, preferred_element_type=jnp.float32)
    grad_features = (own_term + spread.reshape(local_nodes, -1)).astype(jnp.bfloat16)
    return (activated, grad_features, grad_self, grad_neigh)


def solution(mesh):
    return jax.shard_map(
        on_device,
        mesh=mesh,
        in_specs=(
            P(("grp", "blk"), None),
            P(),
            P(),
            P(("grp", "blk"), None),
            P(("grp", "blk"), None, None),
            P(("grp", "blk"), None, None),
            P(("grp", "blk"), None),
            P(("grp", "blk"), None, None, None),
            P(("grp", "blk"), None, None, None),
        ),
        out_specs=(P(("grp", "blk"), None), P(("grp", "blk"), None), P(), P()),
        check_vma=False,
    )
```

profile of v0, /device:TPU:2, one launch (start us, length us, event | category | flops | bytes accessed | tf_op | source)
XLA Modules:
  0.0 803.6 jit_solution(15337653985785510065)
XLA Ops:
  7.2 1.4 copy.27
  8.6 11.6 %all-to-all-start = ((s32[32,1,4]{2,1,0:T(1,128)}), s32[32,1,4]{2,1,0:T(1,128)S(1)}, u32[]{:S(2)}, u32[]{:S(2)}) async-start(s32[32,1,4]{2,1,0:T(1,128)} %copy.27), calls=%async_computation | async-start | bytes 32768 | tf_op jit(solution)/shard_map/all_to_all | solution.py:38
  21.7 1.0 compare_select_fusion
  22.9 1.1 bitcast_select_fusion
  24.0 5.2 convert_reduce_fusion
  29.2 85.8 %gather_fusion = bf16[24576,128]{1,0:T(8,128)(2,1)} fusion(bf16[2048,128]{1,0:T(8,128)(2,1)S(1)} %copy-done, s32[24576]{0:T(1024)S(1)} %broadcast_clamp_fusion), kind=kCustom, calls=%fused_computation | custom fusion | bytes 12681216 | tf_op jit(solution)/shard_map/gather | solution.py:29
  115.0 9.8 %all-to-all-start.2 = ((f32[32,4,128]{2,1,0:T(4,128)}), f32[32,4,128]{2,1,0:T(4,128)S(1)}, u32[]{:S(2)}, u32[]{:S(2)}) async-start(f32[32,4,128]{2,1,0:T(4,128)} %convert_reduce_fusion), calls=%async_computation.3 | async-start | bytes 131072 | tf_op jit(solution)/shard_map/all_to_all | solution.py:37
  124.8 12.8 %fusion.2 = f32[32,4,128,128]{3,2,1,0:T(8,128)} fusion(bf16[32,4,192,128]{3,2,1,0:T(8,128)(2,1)} %bitcast.54, s32[32,4,192]{2,1,0:T(4,128)S(1)} %get-tuple-element.21, pred[32,4]{1,0:T(8,128)(4,1)S(1)} %iota_compare_fusion.9), kind=kOutput, calls=%fused_computation.10 | convolution fusion | flops 811597824 | bytes 14778496 | tf_op jit(solution)/shard_map/oceb,ocef->ocbf/dot_general | solution.py:31
  137.6 9.8 %all-to-all-start.1 = ((f32[32,4,128,128]{3,2,1,0:T(8,128)}), f32[32,4,128,128]{3,2,1,0:T(8,128)}, u32[]{:S(2)}, u32[]{:S(2)}) async-start(f32[32,4,128,128]{3,2,1,0:T(8,128)} %fusion.2), calls=%async_computation.1 | async-start | bytes 16777216 | tf_op jit(solution)/shard_map/all_to_all | solution.py:36
  148.8 1.6 scatter_custom_fusion.1
  150.4 178.8 %all-to-all-done.1 = f32[32,4,128,128]{3,2,1,0:T(8,128)} async-done(((f32[32,4,128,128]{3,2,1,0:T(8,128)}), f32[32,4,128,128]{3,2,1,0:T(8,128)}, u32[]{:S(2)}, u32[]{:S(2)}) %all-to-all-start.1) | async-done | bytes 8388640 | tf_op jit(solution)/shard_map/all_to_all | solution.py:36
  329.3 4.3 broadcast_in_dim.46
  333.5 26.6 %scatter_fusion = f32[128,128,128]{2,1,0:T(8,128)} fusion(f32[128,128,128]{2,1,0:T(8,128)} %broadcast_in_dim.46, s32[128]{0:T(128)S(1)} %reshape.165, f32[128,128,128]{2,1,0:T(8,128)} %bitcast.6), kind=kCustom, calls=%fused_computation.2 | custom fusion | flops 2097152 | bytes 25166336 | tf_op jit(solution)/shard_map/scatter-add | solution.py:42
  360.2 0.8 copy-done.1
  361.0 1.8 fusion.17
  363.4 56.7 %reduce-scatter.3.cloned.1.call-done = f32[16,128,128]{2,1,0:T(8,128)} async-done(((f32[128,128,128]{2,1,0:T(8,128)}), f32[16,128,128]{2,1,0:T(8,128)}) %reduce-scatter.3.cloned.1.call-update) | async-done | bytes 1048592 | tf_op jit(solution)/shard_map/reduce_scatter | solution.py:49
  420.1 1.6 fusion.13
  421.7 4.1 multiply_convert_fusion
  425.8 1.2 fusion.12
  427.4 34.2 %all-gather.2.cloned.1.call-done = bf16[128,128,128]{2,1,0:T(8,128)(2,1)} async-done(((bf16[16,128,128]{2,1,0:T(8,128)(2,1)}), bf16[128,128,128]{2,1,0:T(8,128)(2,1)}) %all-gather.2.cloned.1.call-update) | async-done | bytes 4194320 | tf_op jit(solution)/shard_map/all_gather | solution.py:71
  461.5 5.2 gather_fusion.1
  466.7 10.3 %all-to-all-start.3 = ((bf16[32,4,128,128]{3,2,1,0:T(8,128)(2,1)}), bf16[32,4,128,128]{3,2,1,0:T(8,128)(2,1)}, u32[]{:S(2)}, u32[]{:S(2)}) async-start(bf16[32,4,128,128]{3,2,1,0:T(8,128)(2,1)} %bitcast.53), calls=%async_computation.5 | async-start | bytes 8388608 | tf_op jit(solution)/shard_map/all_to_all | solution.py:75
  477.3 1.2 fusion.18
  478.5 1.1 convolution_bitcast_fusion
  479.8 276.9 %all-reduce.3.cloned.1.call-done = (f32[128,256]{0,1:T(8,128)}, f32[128,256]{0,1:T(8,128)}) async-done(((f32[128,256]{0,1:T(8,128)}, f32[128,256]{0,1:T(8,128)}), (f32[128,256]{0,1:T(8,128)}, f32[128,256]{0,1:T(8,128)})) %all-reduce.3.cloned.1.call-update) | async-done | bytes 262160 | tf_op jit(solution)/shard_map/psum | solution.py:64
  756.8 1.0 broadcast_multiply_fusion
  757.8 0.8 copy.33
  758.5 0.8 copy.34
  759.3 7.3 fusion.39
  766.6 12.1 %fusion.3 = f32[32,4,128,128]{3,2,1,0:T(8,128)} fusion(s32[32,4,192]{2,1,0:T(4,128)S(1)} %get-tuple-element.20, bf16[32,4,192,128]{3,2,1,0:T(8,128)(2,1)S(1)} %fusion.39), kind=kOutput, calls=%fused_computation.11 | convolution fusion | flops 808452096 | bytes 14778368 | tf_op jit(solution)/shard_map/oceb,ocef->ocbf/dot_general | solution.py:80
  778.8 17.0 %scatter_fusion.1 = f32[16,128,128]{2,1,0:T(8,128)S(1)} fusion(f32[16,128,128]{2,1,0:T(8,128)S(1)} %broadcast_in_dim.52, s32[128]{0:T(128)S(1)} %reshape.181, f32[128,128,128]{2,1,0:T(8,128)} %bitcast.52), kind=kCustom, calls=%fused_computation.4 | custom fusion | flops 2097152 | bytes 25166336 | tf_op jit(solution)/shard_map/scatter-add | solution.py:81
  795.9 1.2 fusion.11
  (36 shorter events, 4.7 us)
Async XLA Ops:
  7.2 22.0 %copy-start = (bf16[2048,128]{1,0:T(8,128)(2,1)S(1)}, bf16[2048,128]{1,0:T(8,128)(2,1)}, u32[]{:S(2)}) copy-start(bf16[2048,128]{1,0:T(8,128)(2,1)} %param.9) | copy-start | bytes 1572868
  8.6 106.4 %all-to-all-start = ((s32[32,1,4]{2,1,0:T(1,128)}), s32[32,1,4]{2,1,0:T(1,128)S(1)}, u32[]{:S(2)}, u32[]{:S(2)}) async-start(s32[32,1,4]{2,1,0:T(1,128)} %copy.27), calls=%async_computation | async-start | bytes 32768 | tf_op jit(solution)/shard_map/all_to_all | solution.py:38
  115.0 22.6 %all-to-all-start.2 = ((f32[32,4,128]{2,1,0:T(4,128)}), f32[32,4,128]{2,1,0:T(4,128)S(1)}, u32[]{:S(2)}, u32[]{:S(2)}) async-start(f32[32,4,128]{2,1,0:T(4,128)} %convert_reduce_fusion), calls=%async_computation.3 | async-start | bytes 131072 | tf_op jit(solution)/shard_map/all_to_all | solution.py:37
  137.6 191.7 %all-to-all-start.1 = ((f32[32,4,128,128]{3,2,1,0:T(8,128)}), f32[32,4,128,128]{3,2,1,0:T(8,128)}, u32[]{:S(2)}, u32[]{:S(2)}) async-start(f32[32,4,128,128]{3,2,1,0:T(8,128)} %fusion.2), calls=%async_computation.1 | async-start | bytes 16777216 | tf_op jit(solution)/shard_map/all_to_all | solution.py:36
  147.4 215.3 %reduce-scatter.5.cloned.1.call-start = ((), (), s32[]{:S(2)}) async-start(), calls=%async_computation.7 | async-start | bytes 73728 | tf_op jit(solution)/shard_map/reduce_scatter | solution.py:50
  150.4 269.7 %reduce-scatter.3.cloned.1.call-start = ((), (), s32[]{:S(2)}) async-start(), calls=%async_computation.6 | async-start | bytes 9437184 | tf_op jit(solution)/shard_map/reduce_scatter | solution.py:49
  360.1 0.8 copy-start.1
  360.1 61.6 %copy-start.3 = (bf16[128,256]{1,0:T(8,128)(2,1)S(1)}, bf16[128,256]{1,0:T(8,128)(2,1)}, u32[]{:S(2)}) copy-start(bf16[128,256]{1,0:T(8,128)(2,1)} %param.11) | copy-start | bytes 196612
  360.2 101.4 %all-gather.2.cloned.1.call-start = ((), (), s32[]{:S(2)}) async-start(), calls=%async_computation.8 | async-start | bytes 4718592 | tf_op jit(solution)/shard_map/all_gather | solution.py:71
  466.7 12.9 %copy-start.2 = (s32[1,32,4]{1,2,0:T(4,128)S(1)}, s32[1,32,4]{1,2,0:T(4,128)}, u32[]{:S(2)}) copy-start(s32[1,32,4]{1,2,0:T(4,128)} %param.13) | copy-start | bytes 1540
  466.7 292.6 %all-to-all-start.3 = ((bf16[32,4,128,128]{3,2,1,0:T(8,128)(2,1)}), bf16[32,4,128,128]{3,2,1,0:T(8,128)(2,1)}, u32[]{:S(2)}, u32[]{:S(2)}) async-start(bf16[32,4,128,128]{3,2,1,0:T(8,128)(2,1)} %bitcast.53), calls=%async_computation.5 | async-start | bytes 8388608 | tf_op jit(solution)/shard_map/all_to_all | solution.py:75
  477.1 279.7 %all-reduce.3.cloned.1.call-start = ((), (), s32[]{:S(2)}) async-start(), calls=%async_computation.9 | async-start | bytes 524288 | tf_op jit(solution)/shard_map/psum | solution.py:64
Sparse Core Ops, SparseCore 0:
  151.3 34.6 reduce-scatter.4
  360.3 59.7 reduce-scatter.2
  427.2 34.3 all-gather.1
  484.7 272.0 all-reduce.2
where the time goes:
time: 805 us; the launch traced here: 804 us
  waiting for transfers between devices  547 us (68%)
  local copies, waits for them, and re-layouts  100 us (12%)
  other arithmetic  57.9 us (7%)
  matrix products  42.8 us (5%)
  starting transfers between devices  41.9 us (5%)
  between operations  13.9 us (2%)
    psum x1, waiting for transfers between devices, on_device(): grad_self, grad_neigh = lax.psum((local_self, local_neigh), ('grp', 'blk'))  277 us
    all_to_all x1, waiting for transfers between devices, on_device(): lax.all_to_all(row_sums, 'blk', split_axis=0, concat_axis=0, tiled=True)  179 us
    gather x1, local copies, waits for them, and re-layouts, on_device(): features[src_nodes]  85.8 us
    reduce_scatter x1, waiting for transfers between devices, on_device(): lax.psum_scatter(acc_sums, 'grp', scatter_dimension=0, tiled=True)  56.7 us
    all_gather x1, waiting for transfers between devices, on_device(): lax.all_gather(grad_mean.reshape(local_blocks, block_rows, -1), 'grp', ax...  34.2 us
    scatter-add x1, other arithmetic, on_device(): jax.ops.segment_sum(got_sums.reshape(slot_total, block_rows, -1), targets...  26.6 us
    scatter-add x1, other arithmetic, on_device(): jax.ops.segment_sum(col_sums.reshape(slot_total, block_rows, -1), src_loc...  17 us
  transfers between devices with their start and end apart: 8, of which 4 were waited for; matrix products, arithmetic and copies ran while one was open for 19% of the time, Pallas kernels for 0%

commit v1 on v0

v1 whole, which is shorter than its diff:
```python
import functools

import jax
import jax.numpy as jnp
from jax import lax
from jax.experimental import pallas as pl
from jax.experimental.pallas import tpu as pltpu
from jax.sharding import PartitionSpec as P

BS = 128
PAD = 16
F32 = jnp.float32
BF16 = jnp.bfloat16
VMEM_LIMIT = 48 * 1024 * 1024
NT = (((1,), (1,)), ((), ()))


def dot_nt(a, b):
    return lax.dot_general(a, b, NT, preferred_element_type=F32)


def one_hot_t(row, extent):
    e = row.shape[1]
    ids = lax.broadcasted_iota(jnp.int32, (extent, e), 0)
    return jnp.where(ids == row, 1.0, 0.0).astype(BF16)


def build_kernel(per, cap, src_ref, rows_ref, cols_ref, feat_ref, sum_ref, adj_ref):
    step = pl.program_id(0)
    edges = rows_ref.shape[1]
    for o in range(per):
        counts = jnp.zeros((PAD, BS), F32)
        for c in range(cap):
            s = o * cap + c
            rt = one_hot_t(rows_ref[s : s + 1, :], BS)
            ct = one_hot_t(cols_ref[s : s + 1, :], BS)
            a = dot_nt(rt, ct).astype(BF16)
            adj_ref[s] = dot_nt(ct, rt).astype(BF16)
            x = feat_ref[src_ref[step * per * cap + s]]
            part = jnp.dot(a, x, preferred_element_type=F32)
            sum_ref[o, c * BS : (c + 1) * BS, :] = part.astype(BF16)
            pick = jnp.where(
                lax.broadcasted_iota(jnp.int32, (PAD, edges), 0) == c, 1.0, 0.0
            ).astype(BF16)
            counts = counts + dot_nt(pick, rt)
        sum_ref[o, cap * BS :, :] = counts.astype(BF16)


def build(src, rows, cols, feat, owners, cap):
    per = 4
    slots, edges = rows.shape
    local_blocks = feat.shape[0]
    return pl.pallas_call(
        functools.partial(build_kernel, per, cap),
        grid_spec=pltpu.PrefetchScalarGridSpec(
            num_scalar_prefetch=1,
            grid=(owners // per,),
            in_specs=[
                pl.BlockSpec((per * cap, edges), lambda i, s: (i, 0)),
                pl.BlockSpec((per * cap, edges), lambda i, s: (i, 0)),
                pl.BlockSpec((local_blocks, BS, BS), lambda i, s: (0, 0, 0)),
            ],
            out_specs=[
                pl.BlockSpec((per, cap * BS + PAD, BS), lambda i, s: (i, 0, 0)),
                pl.BlockSpec((per * cap, BS, BS), lambda i, s: (i, 0, 0)),
            ],
        ),
        out_shape=[
            jax.ShapeDtypeStruct((owners, cap * BS + PAD, BS), BF16),
            jax.ShapeDtypeStruct((slots, BS, BS), BF16),
        ],
        compiler_params=pltpu.CompilerParams(vmem_limit_bytes=VMEM_LIMIT),
        cost_estimate=pl.CostEstimate(
            flops=slots * 2 * BS * BS * (2 * edges + BS), bytes_accessed=10 << 20, transcendentals=0
        ),
        name="build",
    )(src, rows, cols, feat)


def gather_kernel(cap, tgt_ref, got_ref, sum_ref, cnt_ref, acc, acc_c):
    targets = sum_ref.shape[0]
    senders = got_ref.shape[0]

    def clear(i, carry):
        acc[i] = jnp.zeros((BS, BS), F32)
        return carry

    lax.fori_loop(0, targets, clear, 0, unroll=4)
    acc_c[...] = jnp.zeros_like(acc_c)

    def add(i, carry):
        for c in range(cap):
            t = tgt_ref[i * cap + c]

            @pl.when(t >= 0)
            def _():
                acc[t] += got_ref[i, c * BS : (c + 1) * BS, :].astype(F32)
                tail = got_ref[i, cap * BS :, :].astype(F32)
                acc_c[pl.ds(t, 1), :] += tail[c : c + 1, :]

        return carry

    lax.fori_loop(0, senders, add, 0)

    def store(i, carry):
        sum_ref[i] = acc[i].astype(BF16)
        return carry

    lax.fori_loop(0, targets, store, 0, unroll=4)
    cnt_ref[...] = acc_c[...]


def gather_sums(tgt, got, targets, cap):
    return pl.pallas_call(
        functools.partial(gather_kernel, cap),
        in_specs=[
            pl.BlockSpec(memory_space=pltpu.SMEM),
            pl.BlockSpec(memory_space=pltpu.VMEM),
        ],
        out_specs=[pl.BlockSpec(memory_space=pltpu.VMEM)] * 2,
        out_shape=[
            jax.ShapeDtypeStruct((targets, BS, BS), BF16),
            jax.ShapeDtypeStruct((targets, BS), F32),
        ],
        scratch_shapes=[pltpu.VMEM((targets, BS, BS), F32), pltpu.VMEM((targets, BS), F32)],
        compiler_params=pltpu.CompilerParams(vmem_limit_bytes=VMEM_LIMIT),
        cost_estimate=pl.CostEstimate(flops=targets * BS * BS, bytes_accessed=10 << 20, transcendentals=0),
        name="gather_sums",
    )(tgt, got)


def spread_kernel(per, src_ref, adj_ref, got_ref, own_ref, out_ref, acc):
    step = pl.program_id(0)

    @pl.when(step == 0)
    def _():
        acc[...] = own_ref[...]

    for s in range(per):
        b = src_ref[step * per + s]
        acc[b] += jnp.dot(adj_ref[s], got_ref[s], preferred_element_type=F32)

    @pl.when(step == pl.num_programs(0) - 1)
    def _():
        out_ref[...] = acc[...].astype(BF16)


def spread(src, adj, got, own):
    per = 16
    slots = adj.shape[0]
    blocks = own.shape[0]
    return pl.pallas_call(
        functools.partial(spread_kernel, per),
        grid_spec=pltpu.PrefetchScalarGridSpec(
            num_scalar_prefetch=1,
            grid=(slots // per,),
            in_specs=[
                pl.BlockSpec((per, BS, BS), lambda i, s: (i, 0, 0)),
                pl.BlockSpec((per, BS, BS), lambda i, s: (i, 0, 0)),
                pl.BlockSpec((blocks, BS, BS), lambda i, s: (0, 0, 0)),
            ],
            out_specs=pl.BlockSpec((blocks, BS, BS), lambda i, s: (0, 0, 0)),
            scratch_shapes=[pltpu.VMEM((blocks, BS, BS), F32)],
        ),
        out_shape=jax.ShapeDtypeStruct((blocks, BS, BS), BF16),
        compiler_params=pltpu.CompilerParams(vmem_limit_bytes=VMEM_LIMIT),
        cost_estimate=pl.CostEstimate(flops=slots * 2 * BS**3, bytes_accessed=10 << 20, transcendentals=0),
        name="spread",
    )(src, adj, got, own)


def on_device(
    features, w_self, w_neigh, cotangent, src_block, dst_block, block_count, edge_rows, edge_cols
):
    owners, cap = src_block.shape[1:]
    edges = edge_rows.shape[-1]
    slots = owners * cap
    local_nodes = features.shape[0]
    local_blocks = local_nodes // BS
    groups = lax.axis_size("grp")
    node_total = local_nodes * groups * owners
    in_use = lax.broadcasted_iota(jnp.int32, (owners, cap), 1) < block_count[0][:, None]
    src = src_block[0].reshape(slots)
    row_ids = jnp.where(in_use[..., None], edge_rows[0], BS).reshape(slots, edges)
    col_ids = jnp.where(in_use[..., None], edge_cols[0], BS).reshape(slots, edges)
    marked = jnp.where(in_use, dst_block[0], -1)
    got_dst = lax.all_to_all(marked, "blk", split_axis=0, concat_axis=0, tiled=True).reshape(slots)
    sums, adj = build(src, row_ids, col_ids, features.reshape(local_blocks, BS, -1), owners, cap)
    got = lax.all_to_all(sums, "blk", split_axis=0, concat_axis=0, tiled=True)
    acc, cnt = gather_sums(got_dst, got, groups * local_blocks, cap)
    own_sums = lax.psum_scatter(acc, "grp", scatter_dimension=0, tiled=True)
    got_cnt = lax.all_to_all(cnt, "grp", split_axis=0, concat_axis=0, tiled=True)
    own_cnt = jnp.sum(got_cnt.reshape(groups, local_blocks, BS), axis=0)
    divisor = jnp.maximum(own_cnt, 1.0).reshape(local_nodes, 1)
    neigh_mean = (own_sums.astype(F32).reshape(local_nodes, -1) / divisor).astype(BF16)
    preact = jnp.dot(features, w_self, preferred_element_type=F32) + jnp.dot(
        neigh_mean, w_neigh, preferred_element_type=F32
    )
    sigmoids = jax.nn.sigmoid(preact)
    activated = (preact * sigmoids).astype(BF16)
    grad_pre = (cotangent.astype(F32) * sigmoids * (1.0 + preact * (1.0 - sigmoids))).astype(BF16)
    grad_mean = (
        jnp.einsum("nh,fh->nf", grad_pre, w_neigh, preferred_element_type=F32) / divisor
    ).astype(BF16)
    mean_all = lax.all_gather(grad_mean.reshape(local_blocks, BS, -1), "grp", axis=0, tiled=True)
    slot_grads = mean_all[jnp.maximum(got_dst, 0)]
    returned = lax.all_to_all(
        slot_grads.reshape(owners, cap, BS, BS), "blk", split_axis=0, concat_axis=0, tiled=True
    )
    both = jnp.concatenate([features, neigh_mean], axis=1)
    grads = jnp.einsum("nf,nh->fh", both, grad_pre, preferred_element_type=F32)
    pieces = lax.all_to_all(grads, "blk", split_axis=0, concat_axis=0, tiled=True)
    piece = jnp.sum(pieces.reshape(owners, grads.shape[0] // owners, -1), axis=0)
    piece = jnp.sum(lax.all_gather(piece, "grp", axis=0, tiled=False), axis=0)
    grads = lax.all_gather(piece, "blk", axis=0, tiled=True) * float(node_total) ** (-0.5)
    own_term = jnp.einsum("nh,fh->nf", grad_pre, w_self, preferred_element_type=F32)
    grad_features = spread(
        src, adj, returned.reshape(slots, BS, BS), own_term.reshape(local_blocks, BS, -1)
    ).reshape(local_nodes, -1)
    f = features.shape[1]
    return (activated, grad_features, grads[:f], grads[f:])


def solution(mesh):
    return jax.shard_map(
        on_device,
        mesh=mesh,
        in_specs=(
            P(("grp", "blk"), None),
            P(),
            P(),
            P(("grp", "blk"), None),
            P(("grp", "blk"), None, None),
            P(("grp", "blk"), None, None),
            P(("grp", "blk"), None),
            P(("grp", "blk"), None, None, None),
            P(("grp", "blk"), None, None, None),
        ),
        out_specs=(P(("grp", "blk"), None), P(("grp", "blk"), None), P(), P()),
        check_vma=False,
    )
```

time: 805 us -> 406 us (0.50)
  waiting for transfers between devices: 547 us -> 150 us
  blocking collectives: 0 us -> 135 us
  local copies, waits for them, and re-layouts: 100 us -> 17.4 us
  other arithmetic: 57.9 us -> 3.74 us
  matrix products: 42.8 us -> 7.94 us
  Pallas kernels: 0 us -> 30 us
    psum x1 -> x0, waiting for transfers between devices: 277 us -> none  [on_device(): grad_self, grad_neigh = lax.psum((local_self, local_neigh), ('grp', 'blk'))]
    all_gather x0 -> x2, blocking collectives: none -> 135 us  [the longest x1 123 us: on_device(): lax.all_gather(piece, 'blk', axis=0, tiled=True)]
    gather x2 -> x1, local copies, waits for them, and re-layouts: 91 us -> 5.22 us  [on_device(): slot_grads = mean_all[jnp.maximum(got_dst, 0)]]
    all_to_all x4 -> x5, waiting for transfers between devices: 179 us -> 99.4 us  [the longest x1 94.3 us: on_device(): got = lax.all_to_all(sums, 'blk', split_axis=0, concat_axis=0, tiled=True)]
    scatter-add x3 -> x0, other arithmetic: 45.3 us -> none  [the longest x1 26.6 us: on_device(): jax.ops.segment_sum(got_sums.reshape(slot_total, block_rows, -1), targets...]
    dot_general x9 -> x5, matrix products: 42.8 us -> 7.94 us  [the longest x1 3.42 us: on_device(): jnp.dot(neigh_mean, w_neigh, preferred_element_type=F32)]
    pallas_call x0 -> x3, Pallas kernels: none -> 30 us  [the longest x1 17 us: build(): pl.pallas_call(functools.partial(build_kernel, per, cap), grid_spec=pltpu...]
    reduce_scatter x2 -> x1, waiting for transfers between devices: 56.7 us -> 29.2 us  [on_device(): own_sums = lax.psum_scatter(acc, 'grp', scatter_dimension=0, tiled=True)]
  transfers between devices with their start and end apart: 8 -> 7, of which waited for: 4 -> 4; matrix products, arithmetic and copies ran while one was open for 19% -> 4% of each run, Pallas kernels for 0% -> 4%
where the time goes in v1:
time: 406 us; the launch traced here: 405 us
  waiting for transfers between devices  150 us (37%)
  blocking collectives  135 us (33%)
  starting transfers between devices  46.6 us (11%)
  Pallas kernels  30 us (7%)
  local copies, waits for them, and re-layouts  17.4 us (4%)
  between operations  14.2 us (3%)
  matrix products  7.94 us (2%)
    all_gather x1, blocking collectives, on_device(): lax.all_gather(piece, 'blk', axis=0, tiled=True)  123 us
    all_to_all x1, waiting for transfers between devices, on_device(): got = lax.all_to_all(sums, 'blk', split_axis=0, concat_axis=0, tiled=True)  94.3 us
    reduce_scatter x1, waiting for transfers between devices, on_device(): own_sums = lax.psum_scatter(acc, 'grp', scatter_dimension=0, tiled=True)  29.2 us
    all_gather x1, waiting for transfers between devices, on_device(): lax.all_gather(grad_mean.reshape(local_blocks, BS, -1), 'grp', axis=0, ti...  21 us
    pallas_call x1, Pallas kernels, build(): pl.pallas_call(functools.partial(build_kernel, per, cap), grid_spec=pltpu...  17 us
    all_gather x1, blocking collectives, on_device(): piece = jnp.sum(lax.all_gather(piece, 'grp', axis=0, tiled=False), axis=0)  12.8 us
    all_to_all x1, starting transfers between devices, on_device(): lax.all_to_all(marked, 'blk', split_axis=0, concat_axis=0, tiled=True)  11.6 us
    all_to_all x1, starting transfers between devices, on_device(): lax.all_to_all(slot_grads.reshape(owners, cap, BS, BS), 'blk', split_axis...  10.3 us
  transfers between devices with their start and end apart: 7, of which 4 were waited for; matrix products, arithmetic and copies ran while one was open for 4% of the time, Pallas kernels for 4%

profile of v1, /device:TPU:2, one launch (start us, length us, event | category | flops | bytes accessed | tf_op | source)
XLA Modules:
  0.0 404.8 jit_solution(2968877891211996856)
XLA Ops:
  7.2 0.7 bitcast_select_fusion
  7.9 0.7 copy.21
  8.6 11.6 %all-to-all-start = ((s32[32,1,4]{2,1,0:T(1,128)}), s32[32,1,4]{2,1,0:T(1,128)S(1)}, u32[]{:S(2)}, u32[]{:S(2)}) async-start(s32[32,1,4]{2,1,0:T(1,128)} %copy.21), calls=%async_computation | async-start | bytes 32768 | tf_op jit(solution)/shard_map/all_to_all | solution.py:187
  20.2 0.7 iota_compare_fusion
  21.1 0.8 copy.22
  21.9 1.0 squeeze.10
  22.9 1.0 squeeze.11
  24.0 1.0 copy-done.4
  25.0 17.0 %build.1 = (bf16[32,528,128]{2,1,0:T(8,128)(2,1)}, bf16[128,128,128]{2,1,0:T(8,128)(2,1)S(1)}) custom-call(s32[128]{0:T(128)S(1)} %reshape_squeeze.3.src_ref, s32[128,192]{1,0:T(8,128)S(1)} %get-tuple-element.19.rows_ref, s32[128,192]{1,0:T(8,128)S(1)} %get-tuple-element.18.cols_ref, bf16[16,128,128]{2,1,0:T(8,128)(2,1)S(1)} %bitcast.29), custom_call_target="tpu_custom_call" | custom-call | flops 2147483648 | bytes 10485760 | tf_op jit(solution)/shard_map/build/pallas_call | solution.py:53
  42.0 2.0 copy-done.1
  44.0 9.8 %all-to-all-start.1 = ((bf16[32,528,128]{2,1,0:T(8,128)(2,1)}), bf16[32,528,128]{2,1,0:T(8,128)(2,1)}, u32[]{:S(2)}, u32[]{:S(2)}) async-start(bf16[32,528,128]{2,1,0:T(8,128)(2,1)} %get-tuple-element.8), calls=%async_computation.1 | async-start | bytes 8650752 | tf_op jit(solution)/shard_map/all_to_all | solution.py:189
  53.9 0.5 broadcast.73
  54.4 0.7 maximum_reduce_fusion
  55.2 94.3 %all-to-all-done.1.got_ref = bf16[32,528,128]{2,1,0:T(8,128)(2,1)} async-done(((bf16[32,528,128]{2,1,0:T(8,128)(2,1)}), bf16[32,528,128]{2,1,0:T(8,128)(2,1)}, u32[]{:S(2)}, u32[]{:S(2)}) %all-to-all-start.1) | async-done | bytes 4325408 | tf_op jit(solution)/shard_map/all_to_all | solution.py:189
  149.5 5.6 %gather_sums.1 = (bf16[128,128,128]{2,1,0:T(8,128)(2,1)S(1)}, f32[128,128]{1,0:T(8,128)}) custom-call(s32[128]{0:T(128)S(1)} %reshape.138.tgt_ref, bf16[32,528,128]{2,1,0:T(8,128)(2,1)} %all-to-all-done.1.got_ref), custom_call_target="tpu_custom_call" | custom-call | flops 2097152 | bytes 10485760 | tf_op jit(solution)/shard_map/gather_sums/pallas_call | solution.py:114
  155.2 1.9 copy-done.3
  157.1 4.6 %all-to-all-start.2 = ((f32[8,16,128]{2,1,0:T(8,128)}), f32[8,16,128]{2,1,0:T(8,128)S(1)}, u32[]{:S(2)}, u32[]{:S(2)}) async-start(f32[8,16,128]{2,1,0:T(8,128)} %bitcast.4), calls=%async_computation.3 | async-start | bytes 131072 | tf_op jit(solution)/shard_map/all_to_all | solution.py:192
  162.2 5.1 %all-to-all-done.2 = f32[8,16,128]{2,1,0:T(8,128)S(1)} async-done(((f32[8,16,128]{2,1,0:T(8,128)}), f32[8,16,128]{2,1,0:T(8,128)S(1)}, u32[]{:S(2)}, u32[]{:S(2)}) %all-to-all-start.2) | async-done | bytes 65568 | tf_op jit(solution)/shard_map/all_to_all | solution.py:192
  167.4 29.2 %reduce-scatter.2.cloned.1.call-done = bf16[16,128,128]{2,1,0:T(8,128)(2,1)} async-done(((bf16[128,128,128]{2,1,0:T(8,128)(2,1)}), bf16[16,128,128]{2,1,0:T(8,128)(2,1)}) %reduce-scatter.2.cloned.1.call-update) | async-done | bytes 524304 | tf_op jit(solution)/shard_map/reduce_scatter | solution.py:191
  196.5 1.4 fusion.4
  197.9 3.4 multiply_convert_fusion
  201.4 1.2 fusion
  202.6 2.4 convolution_bitcast_fusion
  205.1 10.2 %all-to-all-start.4 = ((f32[32,8,256]{2,1,0:T(8,128)}), f32[32,8,256]{2,1,0:T(8,128)S(1)}, u32[]{:S(2)}, u32[]{:S(2)}) async-start(f32[32,8,256]{2,1,0:T(8,128)} %convolution_bitcast_fusion), calls=%async_computation.5 | async-start | bytes 524288 | tf_op jit(solution)/shard_map/all_to_all | solution.py:212
  215.4 21.0 %all-gather.3.cloned.1.call-done = bf16[128,128,128]{2,1,0:T(8,128)(2,1)} async-done(((bf16[16,128,128]{2,1,0:T(8,128)(2,1)}), bf16[128,128,128]{2,1,0:T(8,128)(2,1)}) %all-gather.3.cloned.1.call-update) | async-done | bytes 4194320 | tf_op jit(solution)/shard_map/all_gather | solution.py:205
  236.3 5.2 %gather_fusion = bf16[128,128,128]{2,1,0:T(8,128)(2,1)} fusion(bf16[128,128,128]{2,1,0:T(8,128)(2,1)} %all-gather.3.cloned.1.call-done, s32[1024]{0:T(1024)S(1)} %pad_clamp_fusion), kind=kCustom, calls=%fused_computation | custom fusion | bytes 8389120 | tf_op jit(solution)/shard_map/gather | solution.py:206
  241.6 10.3 %all-to-all-start.3 = ((bf16[32,4,128,128]{3,2,1,0:T(8,128)(2,1)}), bf16[32,4,128,128]{3,2,1,0:T(8,128)(2,1)}, u32[]{:S(2)}, u32[]{:S(2)}) async-start(bf16[32,4,128,128]{3,2,1,0:T(8,128)(2,1)} %bitcast.30), calls=%async_computation.4 | async-start | bytes 8388608 | tf_op jit(solution)/shard_map/all_to_all | solution.py:207
  252.4 12.8 %all-gather = f32[64,256]{1,0:T(8,128)S(1)} all-gather(f32[8,256]{1,0:T(8,128)S(1)} %reduce_sum.28), channel_id=2, replica_groups=mesh['grp'=8,'blk'=32] {'grp'}, dimensions={0}, use_global_device_ids=true | all-gather | bytes 73728 | tf_op jit(solution)/shard_map/all_gather | solution.py:214
  265.1 122.5 %all_gather.15 = f32[256,256]{1,0:T(8,128)S(1)} all-gather(f32[8,256]{1,0:T(8,128)S(1)} %bitcast_reduce_fusion), channel_id=1, replica_groups=mesh['grp'=8,'blk'=32] {'blk'}, dimensions={0}, use_global_device_ids=true | all-gather | bytes 270336 | tf_op jit(solution)/shard_map/all_gather | solution.py:215
  387.7 0.7 fusion.6
  388.4 2.2 copy-done.2
  390.6 7.3 %spread.1 = bf16[16,128,128]{2,1,0:T(8,128)(2,1)} custom-call(s32[128]{0:T(128)S(1)} %reshape_squeeze.3.src_ref, bf16[128,128,128]{2,1,0:T(8,128)(2,1)S(1)} %copy-done.2, bf16[128,128,128]{2,1,0:T(8,128)(2,1)} %bitcast.8.got_ref, f32[16,128,128]{2,1,0:T(8,128)S(1)} %bitcast.28), custom_call_target="tpu_custom_call" | custom-call | flops 536870912 | bytes 10485760 | tf_op jit(solution)/shard_map/spread/pallas_call | solution.py:152
  (34 shorter events, 1.6 us)
Async XLA Ops:
  7.2 190.8 %copy-start = (bf16[128,256]{1,0:T(8,128)(2,1)S(1)}, bf16[128,256]{1,0:T(8,128)(2,1)}, u32[]{:S(2)}) copy-start(bf16[128,256]{1,0:T(8,128)(2,1)} %param.11) | copy-start | bytes 196612
  8.6 35.4 %all-to-all-start = ((s32[32,1,4]{2,1,0:T(1,128)}), s32[32,1,4]{2,1,0:T(1,128)S(1)}, u32[]{:S(2)}, u32[]{:S(2)}) async-start(s32[32,1,4]{2,1,0:T(1,128)} %copy.21), calls=%async_computation | async-start | bytes 32768 | tf_op jit(solution)/shard_map/all_to_all | solution.py:187
  23.9 1.0 copy-start.4
  42.0 2.0 copy-start.1
  44.0 105.5 %all-to-all-start.1 = ((bf16[32,528,128]{2,1,0:T(8,128)(2,1)}), bf16[32,528,128]{2,1,0:T(8,128)(2,1)}, u32[]{:S(2)}, u32[]{:S(2)}) async-start(bf16[32,528,128]{2,1,0:T(8,128)(2,1)} %get-tuple-element.8), calls=%async_computation.1 | async-start | bytes 8650752 | tf_op jit(solution)/shard_map/all_to_all | solution.py:189
  53.8 142.7 %reduce-scatter.2.cloned.1.call-start = ((), (), s32[]{:S(2)}) async-start(), calls=%async_computation.6 | async-start | bytes 4718592 | tf_op jit(solution)/shard_map/reduce_scatter | solution.py:191
  155.2 1.9 copy-start.3
  157.1 4.7 %copy-start.5 = (bf16[2048,128]{1,0:T(8,128)(2,1)S(1)}, bf16[2048,128]{1,0:T(8,128)(2,1)}, u32[]{:S(2)}) copy-start(bf16[2048,128]{1,0:T(8,128)(2,1)} %param.9) | copy-start | bytes 1572868
  157.1 4.7 %copy-start.8 = (bf16[128,256]{1,0:T(8,128)(2,1)S(1)}, bf16[128,256]{1,0:T(8,128)(2,1)}, u32[]{:S(2)}) copy-start(bf16[128,256]{1,0:T(8,128)(2,1)} %param.10) | copy-start | bytes 196612
  157.1 10.2 %all-to-all-start.2 = ((f32[8,16,128]{2,1,0:T(8,128)}), f32[8,16,128]{2,1,0:T(8,128)S(1)}, u32[]{:S(2)}, u32[]{:S(2)}) async-start(f32[8,16,128]{2,1,0:T(8,128)} %bitcast.4), calls=%async_computation.3 | async-start | bytes 131072 | tf_op jit(solution)/shard_map/all_to_all | solution.py:192
  161.7 74.6 %all-gather.3.cloned.1.call-start = ((), (), s32[]{:S(2)}) async-start(), calls=%async_computation.7 | async-start | bytes 4718592 | tf_op jit(solution)/shard_map/all_gather | solution.py:205
  201.4 1.2 copy-start.6
  205.1 36.5 %all-to-all-start.4 = ((f32[32,8,256]{2,1,0:T(8,128)}), f32[32,8,256]{2,1,0:T(8,128)S(1)}, u32[]{:S(2)}, u32[]{:S(2)}) async-start(f32[32,8,256]{2,1,0:T(8,128)} %convolution_bitcast_fusion), calls=%async_computation.5 | async-start | bytes 524288 | tf_op jit(solution)/shard_map/all_to_all | solution.py:212
  241.6 10.3 %copy-start.7 = (bf16[2048,256]{1,0:T(8,128)(2,1)S(1)}, bf16[2048,256]{1,0:T(8,128)(2,1)}, u32[]{:S(2)}) copy-start(bf16[2048,256]{1,0:T(8,128)(2,1)} %copy-done.6) | copy-start | bytes 3145732
  241.6 146.9 %all-to-all-start.3 = ((bf16[32,4,128,128]{3,2,1,0:T(8,128)(2,1)}), bf16[32,4,128,128]{3,2,1,0:T(8,128)(2,1)}, u32[]{:S(2)}, u32[]{:S(2)}) async-start(bf16[32,4,128,128]{3,2,1,0:T(8,128)(2,1)} %bitcast.30), calls=%async_computation.4 | async-start | bytes 8388608 | tf_op jit(solution)/shard_map/all_to_all | solution.py:207
  388.4 2.2 copy-start.2
Sparse Core Ops, SparseCore 0:
  157.3 39.2 reduce-scatter.1
  202.8 33.5 all-gather.2
